TPU v7x, 32 devices: a whole 2x2x4 slice. The times are simulated.
32 devices in a mesh: row: 4 (over y, x), col: 8 (over z, core).
Axes of the slice: x: 2, y: 2, z: 4, core: 2. Of those that a mesh axis runs over, the one named last changes fastest.
Arguments:
- patterns: float32 [8, 16, 256, 256], P('row', 'col'), may hold values from 0.05 to 4
- background: float32 [256, 256], replicated, may hold values from 0.05 to 0.6
- offsets: int32 [8, 16, 2], P('row', 'col'), may hold values from 0 to 64
- probe_wave: float32 [2, 256, 256], replicated, may hold values from -21 to 21
- object_field: float32 [2, 512, 1024], P(None, 'row', 'col'), may hold values from -15 to 15
Outputs:
- new_object: float32 [2, 512, 1024], P(None, 'row', 'col')
- new_probe: float32 [2, 256, 256], replicated
All inputs are finite; a program needn't handle non-finite values.
Results may differ from a plain program's by a relative error of at most 0.0085.
The roundings to bfloat16 on the way count: a program that leaves them out, or rounds other values in their place, can miss the bound.
Values sent between devices are 32-bit elements; how exact they have to be, the bound alone decides.
A program may use at most 64 MiB of HBM per device.

v0:
```python
import math

import jax
import jax.numpy as jnp
from jax import lax
from jax.sharding import PartitionSpec as P

STEP = 64
ITERS = 2


def extended(shard, sides, width):
    for axis, dim in sides:
        count, length = (lax.axis_size(axis), shard.shape[dim])
        up = [(i, (i + 1) % count) for i in range(count - 1)]
        down = [(j, i) for i, j in up]
        last = lax.slice_in_dim(shard, length - width, length, axis=dim)
        first = lax.slice_in_dim(shard, 0, width, axis=dim)
        before = lax.ppermute(last, axis, up)
        after = lax.ppermute(first, axis, down)
        shard = jnp.concatenate([before, shard, after], axis=dim)
    return shard


def dft_tables(side_len):
    indices = jnp.arange(side_len, dtype=jnp.int32)
    phases = indices[:, None] * indices[None, :] % side_len
    angles = phases.astype(jnp.float32) * jnp.float32(2.0 * math.pi / side_len)
    scaling = jnp.float32(1.0 / math.sqrt(side_len))
    return (
        (jnp.cos(angles) * scaling).astype(jnp.bfloat16),
        (-jnp.sin(angles) * scaling).astype(jnp.bfloat16),
    )


def block_tables(real_part, imag_part):
    left_table = jnp.stack([jnp.stack([real_part, -imag_part]), jnp.stack([imag_part, real_part])])
    right_table = jnp.stack([jnp.stack([real_part, imag_part]), jnp.stack([-imag_part, real_part])])
    return (left_table, right_table)


def product(leading, trailing):
    real_part = (
        leading[..., 0, :, :] * trailing[..., 0, :, :]
        - leading[..., 1, :, :] * trailing[..., 1, :, :]
    )
    imag_part = (
        leading[..., 0, :, :] * trailing[..., 1, :, :]
        + leading[..., 1, :, :] * trailing[..., 0, :, :]
    )
    return jnp.stack([real_part, imag_part], axis=-3)


def times_conj(leading, trailing):
    real_part = (
        leading[..., 0, :, :] * trailing[..., 0, :, :]
        + leading[..., 1, :, :] * trailing[..., 1, :, :]
    )
    imag_part = (
        leading[..., 0, :, :] * trailing[..., 1, :, :]
        - leading[..., 1, :, :] * trailing[..., 0, :, :]
    )
    return jnp.stack([real_part, imag_part], axis=-3)


def transform(wave_set, left_table, right_table):
    half_way = jnp.einsum(
        "cdkj,pdjn->pckn", left_table, wave_set, preferred_element_type=jnp.float32
    ).astype(jnp.bfloat16)
    return jnp.einsum("pckn,cdnm->pdkm", half_way, right_table, preferred_element_type=jnp.float32)


def fold_edges(intersection, margin):
    col_rims = jnp.concatenate([intersection[:, :, :margin], intersection[:, :, -margin:]], axis=2)
    col_got = extended(col_rims, (("col", 2),), margin)
    middle = intersection[:, :, margin:-margin]
    middle = middle.at[:, :, :margin].add(col_got[:, :, :margin])
    middle = middle.at[:, :, -margin:].add(col_got[:, :, -margin:])
    row_rims = jnp.concatenate([middle[:, :margin], middle[:, -margin:]], axis=1)
    row_got = extended(row_rims, (("row", 1),), margin)
    centre = middle[:, margin:-margin]
    centre = centre.at[:, :margin].add(row_got[:, :margin])
    centre = centre.at[:, -margin:].add(row_got[:, -margin:])
    return centre


def on_device(patterns, background, offsets, probe_wave, object_field):
    side_len = probe_wave.shape[-1]
    margin = side_len // 2
    pos_rows = patterns.shape[0]
    pos_cols = patterns.shape[1]
    pos_count = pos_rows * pos_cols
    channel_zero = jnp.int32(0)
    real_part, imag_part = dft_tables(side_len)
    forward = block_tables(real_part, imag_part)
    inverse = block_tables(real_part, -imag_part)
    start_rows = (jnp.arange(pos_rows, dtype=jnp.int32)[:, None] * STEP + offsets[:, :, 0]).reshape(
        pos_count
    )
    start_cols = (jnp.arange(pos_cols, dtype=jnp.int32)[None, :] * STEP + offsets[:, :, 1]).reshape(
        pos_count
    )
    amplitude = jnp.sqrt(
        jnp.maximum(patterns.reshape(pos_count, side_len, side_len) - background, 0.0)
    )
    for step_number in range(ITERS):
        widened = extended(object_field, (("row", 1), ("col", 2)), margin)

        def cut_window(row_start, col_start):
            return lax.dynamic_slice(
                widened, (channel_zero, row_start, col_start), (2, side_len, side_len)
            )

        windows = jax.vmap(cut_window)(start_rows, start_cols)
        exit_wave = product(probe_wave, windows)
        far_field = transform(exit_wave.astype(jnp.bfloat16), forward[0], forward[1])
        magnitude = jnp.sqrt(far_field[:, 0] * far_field[:, 0] + far_field[:, 1] * far_field[:, 1])
        projected = (far_field * (amplitude / jnp.maximum(magnitude, 0.5))[:, None]).astype(
            jnp.bfloat16
        )
        back_wave = transform(projected, inverse[0], inverse[1])
        difference = back_wave - exit_wave
        object_terms = times_conj(probe_wave, difference)
        probe_terms = jnp.sum(times_conj(windows, difference), axis=0)
        illumination = probe_wave[0] * probe_wave[0] + probe_wave[1] * probe_wave[1]

        def add_window(position, accumulated):
            row_start = start_rows[position]
            col_start = start_cols[position]
            current = lax.dynamic_slice(
                accumulated, (channel_zero, row_start, col_start), (3, side_len, side_len)
            )
            obj_term = jnp.concatenate([object_terms[position], illumination[None]], axis=0)
            return lax.dynamic_update_slice(
                accumulated, current + obj_term, (channel_zero, row_start, col_start)
            )

        intersection = lax.fori_loop(
            0,
            pos_count,
            add_window,
            jnp.zeros((3, widened.shape[1], widened.shape[2]), jnp.float32),
        )
        folded = fold_edges(intersection, margin)
        light_sum = folded[2]
        summed = lax.psum(probe_terms, ("row", "col"))
        spread = jnp.sqrt(jnp.mean(summed * summed) + 1e-06)
        new_probe = probe_wave + summed / spread
        object_field = object_field + folded[0:2] / (light_sum + 1.0)
        probe_wave = new_probe
    return (object_field, probe_wave)


def solution(mesh):
    placed = (P("row", "col", None, None), P(), P("row", "col", None), P(), P(None, "row", "col"))
    return jax.shard_map(
        on_device,
        mesh=mesh,
        in_specs=placed,
        out_specs=(P(None, "row", "col"), P()),
        check_vma=False,
    )
```

profile of v0, /device:TPU:1, one launch (start us, length us, event | category | flops | bytes accessed | tf_op | source)
XLA Modules:
  0.0 566.5 jit_solution(11492713061421380625)
XLA Ops:
  7.2 4.1 collective-permute-start
  18.7 4.3 collective-permute-start.2
  23.1 1.9 collective-permute-start.3
  33.5 14.0 %while.46 = (s32[]{:T(128)}, f32[2,384,384]{2,1,0:T(8,128)}, s32[4,3]{1,0:T(4,128)S(1)}, f32[4,2,256,256]{2,3,1,0:T(8,128)S(1)}, s32[]{:T(128)}) while((s32[]{:T(128)}, f32[2,384,384]{2,1,0:T(8,128)}, s32[4,3]{1,0:T(4,128)S(1)}, f32[4,2,256,256]{2,3,1,0:T(8,128)S(1)}, s32[]{:T(128)}) %tuple.175), condition=%wide.while_cond.8, body=%wide.while_body.8.sunk | while | flops 2 | bytes 3145845 | solution.py:110
  34.1 2.6 dynamic-slice_bitcast_fusion.4
  37.6 2.6 dynamic-slice_bitcast_fusion.4
  41.1 2.6 dynamic-slice_bitcast_fusion.4
  44.6 2.6 dynamic-slice_bitcast_fusion.4
  47.5 2.6 multiply_subtract_fusion.5
  50.1 4.5 convolution_bitcast_fusion.1
  54.6 3.4 fusion.21
  58.0 5.4 bitcast_subtract_fusion.1
  63.5 3.5 multiply_add_fusion.3
  68.7 71.7 %while.44 = (s32[]{:T(128)}, f32[3,384,384]{2,1,0:T(8,128)S(1)}, s32[4]{0:T(128)S(1)}, s32[4]{0:T(128)S(1)}, f32[4,2,256,256]{2,3,1,0:T(8,128)}, /*index=5*/f32[...) while((s32[]{:T(128)}, f32[3,384,384]{2,1,0:T(8,128)S(1)}, s32[4]{0:T(128)S(1)}, s32[4]{0:T(128)S(1)}, ...), condition=%wide.region_1.2_spmd, body=%wide.region_0.1_spmd.sunk | while | flops 393224 | bytes 6029513 | solution.py:138
  75.4 11.3 %dynamic_update_slice.16 = f32[3,384,384]{2,1,0:T(8,128)S(1)} dynamic-update-slice(f32[3,384,384]{2,1,0:T(8,128)S(1)} %get-tuple-element.701, f32[3,256,256]{2,1,0:T(8,128)S(1)} %maximum_add_fusion.4, s32[]{:T(128)} %constant.337.clone.1..sunk, s32[]{:T(128)S(6)} %select_n.125, s32[]{:T(128)S(6)} %select_n.126) | dynamic-update-slice | bytes 1572868 | tf_op jit(solution)/shard_map/while/body/eval_jaxpr/dynamic_update_slice | solution.py:134
  93.4 12.0 %dynamic_update_slice.16 = f32[3,384,384]{2,1,0:T(8,128)S(1)} dynamic-update-slice(f32[3,384,384]{2,1,0:T(8,128)S(1)} %get-tuple-element.701, f32[3,256,256]{2,1,0:T(8,128)S(1)} %maximum_add_fusion.4, s32[]{:T(128)} %constant.337.clone.1..sunk, s32[]{:T(128)S(6)} %select_n.125, s32[]{:T(128)S(6)} %select_n.126) | dynamic-update-slice | bytes 1572868 | tf_op jit(solution)/shard_map/while/body/eval_jaxpr/dynamic_update_slice | solution.py:134
  112.1 10.4 %dynamic_update_slice.16 = f32[3,384,384]{2,1,0:T(8,128)S(1)} dynamic-update-slice(f32[3,384,384]{2,1,0:T(8,128)S(1)} %get-tuple-element.701, f32[3,256,256]{2,1,0:T(8,128)S(1)} %maximum_add_fusion.4, s32[]{:T(128)} %constant.337.clone.1..sunk, s32[]{:T(128)S(6)} %select_n.125, s32[]{:T(128)S(6)} %select_n.126) | dynamic-update-slice | bytes 1572868 | tf_op jit(solution)/shard_map/while/body/eval_jaxpr/dynamic_update_slice | solution.py:134
  129.2 11.2 %dynamic_update_slice.16 = f32[3,384,384]{2,1,0:T(8,128)S(1)} dynamic-update-slice(f32[3,384,384]{2,1,0:T(8,128)S(1)} %get-tuple-element.701, f32[3,256,256]{2,1,0:T(8,128)S(1)} %maximum_add_fusion.4, s32[]{:T(128)} %constant.337.clone.1..sunk, s32[]{:T(128)S(6)} %select_n.125, s32[]{:T(128)S(6)} %select_n.126) | dynamic-update-slice | bytes 1572868 | tf_op jit(solution)/shard_map/while/body/eval_jaxpr/dynamic_update_slice | solution.py:134
  141.3 2.0 collective-permute-start.4
  143.3 2.4 collective-permute-start.5
  146.7 3.7 collective-permute-done.4
  150.4 4.4 collective-permute-done.5
  156.0 4.0 collective-permute-start.6
  161.5 114.4 %all-reduce.3.cloned.1.call-done = f32[2,256,256]{1,2,0:T(8,128)} async-done(((f32[2,256,256]{1,2,0:T(8,128)}), f32[2,256,256]{1,2,0:T(8,128)}) %all-reduce.3.cloned.1.call-update) | async-done | bytes 524304 | tf_op jit(solution)/shard_map/psum | solution.py:146
  278.6 3.1 collective-permute-start.8
  283.6 5.5 collective-permute-done.9
  289.1 4.2 collective-permute-start.10
  293.3 2.1 collective-permute-start.11
  298.0 4.4 collective-permute-done.11
  303.7 14.1 %while.47 = (s32[]{:T(128)}, f32[2,384,384]{2,1,0:T(8,128)}, s32[4,3]{1,0:T(4,128)S(1)}, f32[4,2,256,256]{2,3,1,0:T(8,128)S(1)}, s32[]{:T(128)}) while((s32[]{:T(128)}, f32[2,384,384]{2,1,0:T(8,128)}, s32[4,3]{1,0:T(4,128)S(1)}, f32[4,2,256,256]{2,3,1,0:T(8,128)S(1)}, s32[]{:T(128)}) %tuple.191), condition=%wide.while_cond.9, body=%wide.while_body.9.sunk | while | flops 2 | bytes 3145845 | solution.py:110
  304.4 2.6 dynamic-slice_bitcast_fusion.5
  307.9 2.6 dynamic-slice_bitcast_fusion.5
  311.4 2.6 dynamic-slice_bitcast_fusion.5
  314.9 2.6 dynamic-slice_bitcast_fusion.5
  317.8 2.6 multiply_subtract_fusion.2
  320.4 4.5 convolution_bitcast_fusion
  324.9 3.4 fusion.16
  328.3 5.4 bitcast_subtract_fusion
  333.7 3.5 multiply_add_fusion
  338.9 69.6 %while.45 = (s32[]{:T(128)}, f32[3,384,384]{2,1,0:T(8,128)S(1)}, s32[4]{0:T(128)S(1)}, s32[4]{0:T(128)S(1)}, f32[4,2,256,256]{2,3,1,0:T(8,128)}, /*index=5*/f32[...) while((s32[]{:T(128)}, f32[3,384,384]{2,1,0:T(8,128)S(1)}, s32[4]{0:T(128)S(1)}, s32[4]{0:T(128)S(1)}, ...), condition=%wide.region_6.7_spmd, body=%wide.region_5.6_spmd.sunk | while | flops 393224 | bytes 6029513 | solution.py:138
  345.1 11.3 %dynamic_update_slice.17 = f32[3,384,384]{2,1,0:T(8,128)S(1)} dynamic-update-slice(f32[3,384,384]{2,1,0:T(8,128)S(1)} %get-tuple-element.743, f32[3,256,256]{2,1,0:T(8,128)S(1)} %maximum_add_fusion.5, s32[]{:T(128)} %constant.337.clone.1..sunk.1, s32[]{:T(128)S(6)} %select_n.127, s32[]{:T(128)S(6)} %select_n.128) | dynamic-update-slice | bytes 1572868 | tf_op jit(solution)/shard_map/while/body/eval_jaxpr/dynamic_update_slice | solution.py:134
  362.6 12.0 %dynamic_update_slice.17 = f32[3,384,384]{2,1,0:T(8,128)S(1)} dynamic-update-slice(f32[3,384,384]{2,1,0:T(8,128)S(1)} %get-tuple-element.743, f32[3,256,256]{2,1,0:T(8,128)S(1)} %maximum_add_fusion.5, s32[]{:T(128)} %constant.337.clone.1..sunk.1, s32[]{:T(128)S(6)} %select_n.127, s32[]{:T(128)S(6)} %select_n.128) | dynamic-update-slice | bytes 1572868 | tf_op jit(solution)/shard_map/while/body/eval_jaxpr/dynamic_update_slice | solution.py:134
  380.8 10.4 %dynamic_update_slice.17 = f32[3,384,384]{2,1,0:T(8,128)S(1)} dynamic-update-slice(f32[3,384,384]{2,1,0:T(8,128)S(1)} %get-tuple-element.743, f32[3,256,256]{2,1,0:T(8,128)S(1)} %maximum_add_fusion.5, s32[]{:T(128)} %constant.337.clone.1..sunk.1, s32[]{:T(128)S(6)} %select_n.127, s32[]{:T(128)S(6)} %select_n.128) | dynamic-update-slice | bytes 1572868 | tf_op jit(solution)/shard_map/while/body/eval_jaxpr/dynamic_update_slice | solution.py:134
  397.3 11.2 %dynamic_update_slice.17 = f32[3,384,384]{2,1,0:T(8,128)S(1)} dynamic-update-slice(f32[3,384,384]{2,1,0:T(8,128)S(1)} %get-tuple-element.743, f32[3,256,256]{2,1,0:T(8,128)S(1)} %maximum_add_fusion.5, s32[]{:T(128)} %constant.337.clone.1..sunk.1, s32[]{:T(128)S(6)} %select_n.127, s32[]{:T(128)S(6)} %select_n.128) | dynamic-update-slice | bytes 1572868 | tf_op jit(solution)/shard_map/while/body/eval_jaxpr/dynamic_update_slice | solution.py:134
  411.6 2.4 collective-permute-start.13
  415.1 127.2 %all-reduce.5.cloned.1.call-done = f32[2,256,256]{1,2,0:T(8,128)} async-done(((f32[2,256,256]{1,2,0:T(8,128)}), f32[2,256,256]{1,2,0:T(8,128)}) %all-reduce.5.cloned.1.call-update) | async-done | bytes 524304 | tf_op jit(solution)/shard_map/psum | solution.py:146
  547.0 3.1 collective-permute-start.14
  552.7 6.2 %collective-permute-done.15 = f32[3,128,128]{2,1,0:T(8,128)S(1)} collective-permute-done((f32[3,128,128]{2,1,0:T(8,128)S(1)}, f32[3,128,128]{2,1,0:T(8,128)S(1)}, u32[]{:S(2)}, u32[]{:S(2)}) %collective-permute-start.15) | collective-permute-done | bytes 196640 | tf_op jit(solution)/shard_map/ppermute | solution.py:20
  (186 shorter events, 71.8 us)
Async XLA Ops:
  7.2 20.0 %copy-start.12 = (f32[2,2,256,256]{3,2,1,0:T(8,128)S(1)}, f32[2,2,256,256]{3,2,1,0:T(8,128)}, u32[]{:S(2)}) copy-start(f32[2,2,256,256]{3,2,1,0:T(8,128)} %param.41) | copy-start | bytes 3145732
  7.2 268.8 %all-reduce.3.cloned.1.call-start = ((), (), s32[]{:S(2)}) async-start(), calls=%async_computation | async-start | bytes 1048576 | tf_op jit(solution)/shard_map/psum | solution.py:146
  7.2 10.0 %collective-permute-start = (f32[2,128,128]{2,1,0:T(8,128)}, f32[2,128,128]{2,1,0:T(8,128)S(1)}, u32[]{:S(2)}, u32[]{:S(2)}) collective-permute-start(f32[2,128,128]{2,1,0:T(8,128)} %param.45), channel_id=1, source_target_pairs={{0,8},{8,16},{16,24},{1,9},{9,17},{17,25},{2,10},{10,18},{18,26},{... | collective-permute-start | bytes 393224 | tf_op jit(solution)/shard_map/ppermute | solution.py:19
  11.3 7.4 %collective-permute-start.1 = (f32[2,128,128]{2,1,0:T(8,128)}, f32[2,128,128]{2,1,0:T(8,128)S(1)}, u32[]{:S(2)}, u32[]{:S(2)}) collective-permute-start(f32[2,128,128]{2,1,0:T(8,128)} %param.45), channel_id=1, source_target_pairs={{8,0},{16,8},{24,16},{9,1},{17,9},{25,17},{10,2},{18,10},{26,18},{... | collective-permute-start | bytes 393224 | tf_op jit(solution)/shard_map/ppermute | solution.py:20
  16.1 12.4 %copy-start.15 = (f32[256,256]{1,0:T(8,128)S(1)}, f32[256,256]{1,0:T(8,128)}, u32[]{:S(2)}) copy-start(f32[256,256]{1,0:T(8,128)} %param.42) | copy-start | bytes 786436
  18.7 11.7 %collective-permute-start.2 = (f32[2,384,128]{2,1,0:T(8,128)S(1)}, f32[2,384,128]{2,1,0:T(8,128)S(1)}, u32[]{:S(2)}, u32[]{:S(2)}) collective-permute-start(f32[2,384,128]{2,1,0:T(8,128)S(1)} %constant_dynamic-update-slice_fusion.2), channel_id=1, source_target_pairs={{0,1},{1,2},{2,3},{3,4},{4,5},{5,6},{6,7},{8,9},{9,10},{10,11},{11... | collective-permute-start | bytes 1179656 | tf_op jit(solution)/shard_map/ppermute | solution.py:19
  23.1 9.1 %collective-permute-start.3 = (f32[2,384,128]{2,1,0:T(8,128)S(1)}, f32[2,384,128]{2,1,0:T(8,128)S(1)}, u32[]{:S(2)}, u32[]{:S(2)}) collective-permute-start(f32[2,384,128]{2,1,0:T(8,128)S(1)} %constant_dynamic-update-slice_fusion.2), channel_id=1, source_target_pairs={{1,0},{2,1},{3,2},{4,3},{5,4},{6,5},{7,6},{9,8},{10,9},{11,10},{12... | collective-permute-start | bytes 1179656 | tf_op jit(solution)/shard_map/ppermute | solution.py:20
  27.1 3.3 copy-start.4
  50.1 4.5 copy-start
  140.4 5.3 copy-start.8
  140.4 5.3 copy-start.9
  141.3 9.1 %collective-permute-start.4 = (f32[3,384,128]{2,1,0:T(8,128)}, f32[3,384,128]{2,1,0:T(8,128)S(1)}, u32[]{:S(2)}, u32[]{:S(2)}) collective-permute-start(f32[3,384,128]{2,1,0:T(8,128)} %get-tuple-element.524), channel_id=1, source_target_pairs={{0,1},{1,2},{2,3},{3,4},{4,5},{5,6},{6,7},{8,9},{9,10},{10,11},{11... | collective-permute-start | bytes 1769480 | tf_op jit(solution)/shard_map/ppermute | solution.py:19
  143.3 11.5 %collective-permute-start.5 = (f32[3,384,128]{2,1,0:T(8,128)S(1)}, f32[3,384,128]{2,1,0:T(8,128)}, u32[]{:S(2)}, u32[]{:S(2)}) collective-permute-start(f32[3,384,128]{2,1,0:T(8,128)S(1)} %get-tuple-element.525), channel_id=1, source_target_pairs={{1,0},{2,1},{3,2},{4,3},{5,4},{6,5},{7,6},{9,8},{10,9},{11,10},{12... | collective-permute-start | bytes 1769480 | tf_op jit(solution)/shard_map/ppermute | solution.py:20
  146.6 14.6 %copy-start.5 = (f32[2,256,256]{2,1,0:T(8,128)S(1)}, f32[2,256,256]{2,1,0:T(8,128)}, u32[]{:S(2)}) copy-start(f32[2,256,256]{2,1,0:T(8,128)} %param.44) | copy-start | bytes 1572868
  146.7 395.6 %all-reduce.5.cloned.1.call-start = ((), (), s32[]{:S(2)}) async-start(), calls=%async_computation.1 | async-start | bytes 1048576 | tf_op jit(solution)/shard_map/psum | solution.py:146
  155.9 122.6 %copy-start.14 = (f32[2,128,128]{2,1,0:T(8,128)S(1)}, f32[2,128,128]{2,1,0:T(8,128)}, u32[]{:S(2)}) copy-start(f32[2,128,128]{2,1,0:T(8,128)} %param.45) | copy-start | bytes 393220
  156.0 122.5 %collective-permute-start.6 = (f32[3,128,128]{2,1,0:T(8,128)S(1)}, f32[3,128,128]{2,1,0:T(8,128)S(1)}, u32[]{:S(2)}, u32[]{:S(2)}) collective-permute-start(f32[3,128,128]{2,1,0:T(8,128)S(1)} %get-tuple-element.528), channel_id=1, source_target_pairs={{0,8},{8,16},{16,24},{1,9},{9,17},{17,25},{2,10},{10,18},{18,26},{... | collective-permute-start | bytes 589832 | tf_op jit(solution)/shard_map/ppermute | solution.py:19
  160.0 118.5 %collective-permute-start.7 = (f32[3,128,128]{2,1,0:T(8,128)S(1)}, f32[3,128,128]{2,1,0:T(8,128)S(1)}, u32[]{:S(2)}, u32[]{:S(2)}) collective-permute-start(f32[3,128,128]{2,1,0:T(8,128)S(1)} %get-tuple-element.529), channel_id=1, source_target_pairs={{8,0},{16,8},{24,16},{9,1},{17,9},{25,17},{10,2},{18,10},{26,18},{... | collective-permute-start | bytes 589832 | tf_op jit(solution)/shard_map/ppermute | solution.py:20
  275.9 7.1 %copy-start.10 = (f32[2,256,256]{1,2,0:T(8,128)S(1)}, f32[2,256,256]{1,2,0:T(8,128)}, u32[]{:S(2)}) copy-start(f32[2,256,256]{1,2,0:T(8,128)} %all-reduce.3.cloned.1.call-done) | copy-start | bytes 1572868
  278.6 5.0 collective-permute-start.8
  281.7 7.4 %collective-permute-start.9 = (f32[2,128,128]{2,1,0:T(8,128)S(1)}, f32[2,128,128]{2,1,0:T(8,128)S(1)}, u32[]{:S(2)}, u32[]{:S(2)}) collective-permute-start(f32[2,128,128]{2,1,0:T(8,128)S(1)} %fusion.49), channel_id=1, source_target_pairs={{8,0},{16,8},{24,16},{9,1},{17,9},{25,17},{10,2},{18,10},{26,18},{... | collective-permute-start | bytes 393224 | tf_op jit(solution)/shard_map/ppermute | solution.py:20
  283.1 19.3 %copy-start.2 = (f32[2,256,256]{1,2,0:T(8,128)}, f32[2,256,256]{1,2,0:T(8,128)S(1)}, u32[]{:S(2)}) copy-start(f32[2,256,256]{1,2,0:T(8,128)S(1)} %divide_add_fusion.1) | copy-start | bytes 1572868
  289.1 8.9 %collective-permute-start.10 = (f32[2,384,128]{2,1,0:T(8,128)S(1)}, f32[2,384,128]{2,1,0:T(8,128)S(1)}, u32[]{:S(2)}, u32[]{:S(2)}) collective-permute-start(f32[2,384,128]{2,1,0:T(8,128)S(1)} %pad_maximum_fusion.6), channel_id=1, source_target_pairs={{0,1},{1,2},{2,3},{3,4},{4,5},{5,6},{6,7},{8,9},{9,10},{10,11},{11... | collective-permute-start | bytes 1179656 | tf_op jit(solution)/shard_map/ppermute | solution.py:19
  293.3 9.1 %collective-permute-start.11 = (f32[2,384,128]{2,1,0:T(8,128)S(1)}, f32[2,384,128]{2,1,0:T(8,128)S(1)}, u32[]{:S(2)}, u32[]{:S(2)}) collective-permute-start(f32[2,384,128]{2,1,0:T(8,128)S(1)} %pad_maximum_fusion.6), channel_id=1, source_target_pairs={{1,0},{2,1},{3,2},{4,3},{5,4},{6,5},{7,6},{9,8},{10,9},{11,10},{12... | collective-permute-start | bytes 1179656 | tf_op jit(solution)/shard_map/ppermute | solution.py:20
  320.4 4.5 copy-start.1
  408.6 5.5 copy-start.6
  408.6 5.5 copy-start.7
  409.7 135.1 %collective-permute-start.12 = (f32[3,384,128]{2,1,0:T(8,128)}, f32[3,384,128]{2,1,0:T(8,128)S(1)}, u32[]{:S(2)}, u32[]{:S(2)}) collective-permute-start(f32[3,384,128]{2,1,0:T(8,128)} %get-tuple-element.522), channel_id=1, source_target_pairs={{0,1},{1,2},{2,3},{3,4},{4,5},{5,6},{6,7},{8,9},{9,10},{10,11},{11... | collective-permute-start | bytes 1769480 | tf_op jit(solution)/shard_map/ppermute | solution.py:19
  411.6 134.0 %collective-permute-start.13 = (f32[3,384,128]{2,1,0:T(8,128)}, f32[3,384,128]{2,1,0:T(8,128)}, u32[]{:S(2)}, u32[]{:S(2)}) collective-permute-start(f32[3,384,128]{2,1,0:T(8,128)} %get-tuple-element.523), channel_id=1, source_target_pairs={{1,0},{2,1},{3,2},{4,3},{5,4},{6,5},{7,6},{9,8},{10,9},{11,10},{12... | collective-permute-start | bytes 1769480 | tf_op jit(solution)/shard_map/ppermute | solution.py:20
  415.0 136.4 %copy-start.3 = (f32[2,256,256]{1,2,0:T(8,128)S(1)}, f32[2,256,256]{1,2,0:T(8,128)}, u32[]{:S(2)}) copy-start(f32[2,256,256]{1,2,0:T(8,128)} %copy-done.2) | copy-start | bytes 1572868
  542.3 9.2 %copy-start.11 = (f32[2,256,256]{1,2,0:T(8,128)S(1)}, f32[2,256,256]{1,2,0:T(8,128)}, u32[]{:S(2)}) copy-start(f32[2,256,256]{1,2,0:T(8,128)} %all-reduce.5.cloned.1.call-done) | copy-start | bytes 1572868
  544.8 0.8 copy-start.13
  547.0 5.7 %collective-permute-start.14 = (f32[3,128,128]{2,1,0:T(8,128)S(1)}, f32[3,128,128]{2,1,0:T(8,128)S(1)}, u32[]{:S(2)}, u32[]{:S(2)}) collective-permute-start(f32[3,128,128]{2,1,0:T(8,128)S(1)} %get-tuple-element.526), channel_id=1, source_target_pairs={{0,8},{8,16},{16,24},{1,9},{9,17},{17,25},{2,10},{10,18},{18,26},{... | collective-permute-start | bytes 589832 | tf_op jit(solution)/shard_map/ppermute | solution.py:19
  550.1 8.8 %collective-permute-start.15 = (f32[3,128,128]{2,1,0:T(8,128)S(1)}, f32[3,128,128]{2,1,0:T(8,128)S(1)}, u32[]{:S(2)}, u32[]{:S(2)}) collective-permute-start(f32[3,128,128]{2,1,0:T(8,128)S(1)} %get-tuple-element.527), channel_id=1, source_target_pairs={{8,0},{16,8},{24,16},{9,1},{17,9},{25,17},{10,2},{18,10},{26,18},{... | collective-permute-start | bytes 589832 | tf_op jit(solution)/shard_map/ppermute | solution.py:20
Sparse Core Ops, SparseCore 0:
  146.8 129.0 all-reduce.2
  415.2 127.0 all-reduce.4
where the time goes:
time: 570 us; the launch traced here: 566 us
  waiting for transfers between devices  270 us (47%)
  local copies, waits for them, and re-layouts  151 us (26%)
  starting transfers between devices  40.7 us (7%)
  other arithmetic  39 us (7%)
  loops' own time  29.7 us (5%)
  matrix products  19.9 us (3%)
  between operations  16 us (3%)
    psum x2, waiting for transfers between devices, on_device(): summed = lax.psum(probe_terms, ('row', 'col'))  242 us
    dynamic_update_slice x8, local copies, waits for them, and re-layouts, add_window(): lax.dynamic_update_slice(accumulated, current + obj_term, (channel_zero,...  90 us
    another operation x2, loops' own time, on_device(): lax.fori_loop(0, pos_count, add_window, jnp.zeros((3, widened.shape[1], w...  29.4 us
    gather x40, local copies, waits for them, and re-layouts  27.8 us
    ppermute x8, starting transfers between devices, extended(): before = lax.ppermute(last, axis, up)  26.6 us
    ppermute x8, waiting for transfers between devices, extended(): after = lax.ppermute(first, axis, down)  22.7 us
    dot_general x4, matrix products, transform(): jnp.einsum('pckn,cdnm->pdkm', half_way, right_table, preferred_element_ty...  19.9 us
    ppermute x8, starting transfers between devices, extended(): after = lax.ppermute(first, axis, down)  14 us
  transfers between devices with their start and end apart: 18, of which 12 were waited for; matrix products, arithmetic and copies ran while one was open for 4% of the time, Pallas kernels for 0%

commit v1 on v0

v1 whole, which is shorter than its diff:
```python
import functools
import math

import jax
import jax.numpy as jnp
import numpy as np
from jax import lax
from jax.experimental import pallas as pl
from jax.experimental.pallas import tpu as pltpu
from jax.sharding import PartitionSpec as P

STEP = 64
ITERS = 2
LANES = 128
F32 = jnp.float32
BF16 = jnp.bfloat16


def dft_parts(side_len):
    indices = np.arange(side_len, dtype=np.int32)
    phases = indices[:, None] * indices[None, :] % side_len
    angles = phases.astype(np.float32) * np.float32(2.0 * math.pi / side_len)
    scaling = np.float32(1.0 / math.sqrt(side_len))
    real = (np.cos(angles) * scaling).astype(jnp.bfloat16)
    imag = (-np.sin(angles) * scaling).astype(jnp.bfloat16)
    return np.stack([real, imag]).astype(np.float32)


def plan(rows, cols, side):
    half = 2 * side
    pairs = cols // 2
    by_row = half // rows
    by_pair = max(8, by_row // pairs)
    owners = by_row // by_pair
    sems = {"halo": 0, "fold_col": 8, "fold_row": 14, "pair": 20}
    sems["row_sum"] = 21
    sems["col_sum"] = sems["row_sum"] + rows - 1
    sems["col_all"] = sems["col_sum"] + pairs - 1
    sems["row_all"] = sems["col_all"] + pairs - 1
    sems["pair_all"] = sems["row_all"] + rows - 1
    count = sems["pair_all"] + 1
    return half, pairs, by_row, by_pair, owners, sems, count


def kernel(rows, cols, pos_rows, pos_cols, side, *refs):
    inputs, (tile_out, probe_out) = refs[:6], refs[6:8]
    (amp, pad, lpad, win, exit_b, half_b, far, probe) = refs[8:16]
    (patterns, background, offsets, probe_in, tables, left, right, in_sem) = refs[16:24]
    (tile_end, probe_end, out_sem) = refs[24:27]
    per_iter = [refs[27 + 11 * i : 38 + 11 * i] for i in range(ITERS)]
    half, pairs, by_row, by_pair, owners, sems, _ = plan(rows, cols, side)
    margin = side // 2
    wide = 3 * margin
    positions = pos_rows * pos_cols
    row, col = lax.axis_index("row"), lax.axis_index("col")
    parity = lax.rem(col, 2)
    mate = col + 1 - 2 * parity
    group = lax.div(col, 2)
    has_up, has_down = row > 0, row < rows - 1
    has_left, has_right = col > 0, col < cols - 1
    up, down = lax.max(row - 1, 0), lax.min(row + 1, rows - 1)
    before, after = lax.max(col - 1, 0), lax.min(col + 1, cols - 1)
    started = []

    def at(r, c):
        return {"row": r, "col": c}

    def when(cond, act):
        if cond is None:
            act()
        else:
            pl.when(cond)(act)

    def row_pos(d):
        return lax.rem(row + d, rows)

    def pair_pos(d):
        return lax.rem(group + d, pairs)

    barrier = pltpu.get_barrier_semaphore()

    def greet(device):
        pl.semaphore_signal(barrier, inc=1, device_id=device, device_id_type=pl.DeviceIdType.MESH)

    for d in range(1, rows):
        greet(at(row_pos(d), col))
    for d in range(1, pairs):
        greet(at(row, 2 * pair_pos(d) + parity))
    when(has_left, lambda: greet(at(row, before)))
    when(has_right, lambda: greet(at(row, after)))

    def lane_index(n):
        return lax.broadcasted_iota(jnp.int32, (n, LANES), 1)

    def starts(p):
        a, b = lax.div(p, pos_cols), lax.rem(p, pos_cols)
        return a * STEP + offsets[a, b, 0], b * STEP + offsets[a, b, 1]

    def spread_lanes(first, second, c0):
        keep = lane_index(first.shape[0]) >= c0
        turn = lax.rem(c0, LANES)
        first, second = pltpu.roll(first, turn, 1), pltpu.roll(second, turn, 1)
        zero = jnp.zeros_like(first)
        return (
            jnp.where(keep, first, zero),
            jnp.where(keep, second, first),
            jnp.where(keep, zero, second),
        )

    centre = per_iter[0][0].at[:, 1, margin : 2 * margin, :]
    homes = (patterns, background, offsets, probe_in, centre, tables)
    fetches = [pltpu.make_async_copy(a, b, in_sem.at[i]) for i, (a, b) in enumerate(zip(inputs, homes))]
    for i in (4, 3, 2, 0, 1, 5):
        fetches[i].start()
    for wide_ref in (it[0] for it in per_iter):
        zeros = jnp.zeros((2, 3, margin, LANES), F32)

        @pl.when(row == 0)
        def _():
            wide_ref[:, :, 0:margin, :] = zeros

        @pl.when(row == rows - 1)
        def _():
            wide_ref[:, :, 2 * margin : wide, :] = zeros

        @pl.when(col == 0)
        def _():
            wide_ref[:, 0] = jnp.zeros((2, wide, LANES), F32)

        @pl.when(col == cols - 1)
        def _():
            wide_ref[:, 2] = jnp.zeros((2, wide, LANES), F32)

    beside = lax.min(col, 1) + lax.min(cols - 1 - col, 1)
    fetches[4].wait()
    pl.semaphore_wait(barrier, rows - 1 + pairs - 1 + beside)

    def link(step):
        s_sem, r_sem = per_iter[step][9:11]

        def copy(src, dst, k, device):
            return pltpu.make_async_remote_copy(
                src_ref=src,
                dst_ref=dst,
                send_sem=s_sem.at[k],
                recv_sem=r_sem.at[k],
                device_id=device,
                device_id_type=pl.DeviceIdType.MESH,
            )

        def send(src, dst, k, device, cond=None):
            moved = copy(src, dst, k, device)
            when(cond, moved.start)
            started.append((cond, moved))

        def arrive(dst, k, cond=None):
            when(cond, copy(dst, dst, k, at(row, mate)).wait_recv)

        return send, arrive

    def thirds(step):
        return lambda j, s: per_iter[step][0].at[:, j, s * margin : (s + 1) * margin, :]

    def strip_on(step, s, cond):
        send, third = link(step)[0], thirds(step)
        base = sems["halo"] + 2 + s
        go_right = has_right if cond is None else jnp.logical_and(has_right, cond)
        go_left = has_left if cond is None else jnp.logical_and(has_left, cond)
        send(third(1, s), third(0, s), base, at(row, after), go_right)
        send(third(1, s), third(2, s), base + 3, at(row, before), go_left)

    def halo_out(step):
        send, third = link(step)[0], thirds(step)
        send(third(1, 1), third(1, 0), sems["halo"], at(down, col), has_down)
        send(third(1, 1), third(1, 2), sems["halo"] + 1, at(up, col), has_up)
        strip_on(step, 1, None)

    def halo_on(step):
        arrive, third = link(step)[1], thirds(step)
        arrive(third(1, 0), sems["halo"], has_up)
        strip_on(step, 0, has_up)
        arrive(third(1, 2), sems["halo"] + 1, has_down)
        strip_on(step, 2, has_down)

    def halo_end(step):
        arrive, third = link(step)[1], thirds(step)
        for s, cond in ((1, None), (0, has_up), (2, has_down)):
            base = sems["halo"] + 2 + s
            from_left = has_left if cond is None else jnp.logical_and(has_left, cond)
            from_right = has_right if cond is None else jnp.logical_and(has_right, cond)
            arrive(third(0, s), base, from_left)
            arrive(third(2, s), base + 3, from_right)

    for step in range(ITERS):
        wide_ref, acc, got_col, got_row, grad, got_pair, got_rows, got_cols, total, s_sem, r_sem = (
            per_iter[step]
        )
        last = step == ITERS - 1

        send, arrive = link(step)
        third = thirds(step)
        if step == 0:
            halo_out(step)

        if step == 0:
            for i in (0, 1, 2, 3):
                fetches[i].wait()
            for ch in range(2):
                for j in range(2):
                    at_row = (2 * ch + j) * side
                    probe[at_row : at_row + side, :] = probe_in[ch, :, j * LANES : (j + 1) * LANES]

            @pl.loop(0, positions)
            def _(p):
                a, b = lax.div(p, pos_cols), lax.rem(p, pos_cols)
                amp[p] = jnp.sqrt(jnp.maximum(patterns[a, b] - background[...], 0.0))
                edge = jnp.zeros((3, margin, LANES), F32)
                for lo in (0, wide):
                    lpad[p, :, lo : lo + margin, :] = edge
                    for ch in range(2):
                        pad[p, ch, :, lo : lo + margin, :] = edge

        chunk = 32

        @pl.loop(0, positions * (side // chunk))
        def _(i):
            p = lax.div(i, side // chunk)
            r = lax.rem(i, side // chunk) * chunk
            _, c0 = starts(p)
            light = []
            for j in range(2):
                pr = probe[pl.ds(pl.multiple_of(j * side + r, chunk), chunk), :]
                pi = probe[pl.ds(pl.multiple_of((2 + j) * side + r, chunk), chunk), :]
                light.append(pr * pr + pi * pi)
            for j, part in enumerate(spread_lanes(light[0], light[1], c0)):
                lpad[p, j, pl.ds(pl.multiple_of(margin + r, chunk), chunk), :] = part

        def gather(source, to):
            row_starts = [starts(p)[0] for p in range(positions)]

            @pl.loop(0, wide // 64)
            def _(i):
                r = i * 64
                for j in range(3):
                    parts = [source(p, j, pl.ds(margin - row_starts[p] + r, 64)) for p in range(positions)]
                    acc[to, j, pl.ds(pl.multiple_of(r, 64), 64), :] = functools.reduce(
                        lambda x, y: x + y, parts
                    )

        def fold_cols(ch):
            k = sems["fold_col"] + 2 * ch
            send(acc.at[ch, 2], got_col.at[0, ch], k, at(row, after), has_right)
            send(acc.at[ch, 0], got_col.at[1, ch], k + 1, at(row, before), has_left)

        def fold_rows(ch):
            k = sems["fold_col"] + 2 * ch
            for side_at, cond in ((0, has_left), (1, has_right)):
                arrive(got_col.at[side_at, ch], k + side_at, cond)

                @pl.when(cond)
                def _():
                    acc[ch, 1] += got_col[side_at, ch]

            k = sems["fold_row"] + 2 * ch
            send(acc.at[ch, 1, 2 * margin : wide], got_row.at[0, ch], k, at(down, col), has_down)
            send(acc.at[ch, 1, 0:margin], got_row.at[1, ch], k + 1, at(up, col), has_up)

        def fold_end(ch):
            k = sems["fold_row"] + 2 * ch
            for side_at, cond in ((0, has_up), (1, has_down)):
                arrive(got_row.at[side_at, ch], k + side_at, cond)

                @pl.when(cond)
                def _():
                    acc[ch, 1, margin : 2 * margin] += got_row[side_at, ch]

        gather(lambda p, j, rs: lpad[p, j, rs, :], 2)
        fold_cols(2)

        if step == 0:
            halo_on(step)
            fetches[5].wait()
            real, imag = tables[0].astype(BF16), tables[1].astype(BF16)
            less = (-tables[1]).astype(BF16)
            for to, (one, two, three, four) in (
                (left, (real, less, imag, real)),
                (right, (real, imag, less, real)),
            ):
                to[0:side, 0:side] = one
                to[0:side, side : 2 * side] = two
                to[side : 2 * side, 0:side] = three
                to[side : 2 * side, side : 2 * side] = four
        grad[...] = jnp.zeros_like(grad)
        halo_end(step)
        fold_rows(2)

        def probe_part(ch, j, r):
            return probe[pl.ds(pl.multiple_of((2 * ch + j) * side + r, chunk), chunk), :]

        @pl.loop(0, positions)
        def _(p):
            r0, c0 = starts(p)

            @pl.loop(0, side // chunk)
            def _(i):
                r = i * chunk
                rs = pl.ds(pl.multiple_of(r, chunk), chunk)
                inside = lane_index(chunk) < LANES - c0
                turn = lax.rem(2 * LANES - c0, LANES)
                parts = []
                for ch in range(2):
                    b = [
                        pltpu.roll(wide_ref[ch, j, pl.ds(r0 + r, chunk), :], turn, 1)
                        for j in range(3)
                    ]
                    parts.append([jnp.where(inside, b[j], b[j + 1]) for j in range(2)])
                for j in range(2):
                    wr, wi = parts[0][j], parts[1][j]
                    pr, pi = probe_part(0, j, r), probe_part(1, j, r)
                    lanes = slice(j * LANES, (j + 1) * LANES)
                    win[0, rs, lanes] = wr
                    win[1, rs, lanes] = wi
                    exit_b[rs, lanes] = (pr * wr - pi * wi).astype(BF16)
                    ri = pl.ds(pl.multiple_of(side + r, chunk), chunk)
                    exit_b[ri, lanes] = (pr * wi + pi * wr).astype(BF16)

            def transform(one, two):
                halfway = jnp.dot(one[...], exit_b[...], preferred_element_type=F32).astype(BF16)
                half_b[:, 0:side] = halfway[0:side]
                half_b[:, side : 2 * side] = halfway[side : 2 * side]
                far[...] = jnp.dot(half_b[...], two[...], preferred_element_type=F32)

            transform(left, right)

            @pl.loop(0, side // chunk)
            def _(i):
                r = i * chunk
                rs = pl.ds(pl.multiple_of(r, chunk), chunk)
                fr, fi = far[rs, 0:side], far[rs, side : 2 * side]
                scale = amp[p, rs, :] * lax.rsqrt(jnp.maximum(fr * fr + fi * fi, 0.25))
                exit_b[rs, :] = (fr * scale).astype(BF16)
                ri = pl.ds(pl.multiple_of(side + r, chunk), chunk)
                exit_b[ri, :] = (fi * scale).astype(BF16)

            transform(right, left)

            @pl.loop(0, side // chunk)
            def _(i):
                r = i * chunk
                rs = pl.ds(pl.multiple_of(r, chunk), chunk)
                terms = [[], []]
                for j in range(2):
                    lanes = slice(j * LANES, (j + 1) * LANES)
                    wr, wi = win[0, rs, lanes], win[1, rs, lanes]
                    pr, pi = probe_part(0, j, r), probe_part(1, j, r)
                    dr = far[rs, j * LANES : (j + 1) * LANES] - (pr * wr - pi * wi)
                    di = far[rs, side + j * LANES : side + (j + 1) * LANES] - (pr * wi + pi * wr)
                    terms[0].append(pr * dr + pi * di)
                    terms[1].append(pr * di - pi * dr)
                    to_r = pl.ds(pl.multiple_of(j * side + r, chunk), chunk)
                    to_i = pl.ds(pl.multiple_of((2 + j) * side + r, chunk), chunk)
                    grad[to_r, :] += wr * dr + wi * di
                    grad[to_i, :] += wr * di - wi * dr
                for ch in range(2):
                    for j, part in enumerate(spread_lanes(terms[ch][0], terms[ch][1], c0)):
                        pad[p, ch, j, pl.ds(pl.multiple_of(margin + r, chunk), chunk), :] = part

        def span(start, size):
            return pl.ds(pl.multiple_of(start, 8), size)

        mine, theirs = parity * half, (1 - parity) * half
        base_row = mine + row * by_row
        base_own = base_row + group * by_pair
        owns = None if owners == pairs else group < owners

        send(grad.at[span(theirs, half)], got_pair, sems["pair"], at(row, mate))
        for ch in range(2):
            gather(lambda p, j, rs, ch=ch: pad[p, ch, j, rs, :], ch)
            fold_cols(ch)
        arrive(got_pair, sems["pair"])
        grad[span(mine, half), :] += got_pair[...]

        for d in range(1, rows):
            piece = grad.at[span(mine + row_pos(d) * by_row, by_row)]
            send(piece, got_rows.at[d - 1], sems["row_sum"] + d - 1, at(row_pos(d), col))
        fold_rows(0)
        for d in range(1, rows):
            arrive(got_rows.at[d - 1], sems["row_sum"] + d - 1)
        summed = grad[span(base_row, by_row), :]
        for d in range(1, rows):
            summed += got_rows[d - 1]
        grad[span(base_row, by_row), :] = summed

        for d in range(1, pairs):
            to = pair_pos(d)
            cond = None if owners == pairs else to < owners
            piece = grad.at[span(base_row + lax.min(to, owners - 1) * by_pair, by_pair)]
            send(piece, got_cols.at[d - 1], sems["col_sum"] + d - 1, at(row, 2 * to + parity), cond)
        fold_rows(1)
        for d in range(1, pairs):
            arrive(got_cols.at[d - 1], sems["col_sum"] + d - 1, owns)

        def finish():
            own = grad[span(base_own, by_pair), :]
            for d in range(1, pairs):
                own += got_cols[d - 1]
            total[span(base_own, by_pair), :] = own

        when(owns, finish)

        for d in range(1, pairs):
            piece = total.at[span(base_row + lax.min(group, owners - 1) * by_pair, by_pair)]
            device = at(row, 2 * pair_pos(d) + parity)
            send(piece, piece, sems["col_all"] + d - 1, device, owns)

        middle = slice(margin, 2 * margin)
        fold_end(2)
        for ch in range(2):
            fold_end(ch)
            changed = wide_ref[ch, 1, middle] + acc[ch, 1, middle] / (acc[2, 1, middle] + 1.0)
            if last:
                tile_end[ch] = changed
            else:
                per_iter[step + 1][0][ch, 1, middle] = changed
        if last:
            leaving = pltpu.make_async_copy(tile_end, tile_out, out_sem.at[0])
            leaving.start()
        else:
            halo_out(step + 1)

        for d in range(1, pairs):
            origin = pair_pos(pairs - d)
            cond = None if owners == pairs else origin < owners
            piece = total.at[span(base_row + lax.min(origin, owners - 1) * by_pair, by_pair)]
            arrive(piece, sems["col_all"] + d - 1, cond)
        for d in range(1, rows):
            piece = total.at[span(base_row, by_row)]
            send(piece, piece, sems["row_all"] + d - 1, at(row_pos(d), col))
        for d in range(1, rows):
            piece = total.at[span(mine + row_pos(rows - d) * by_row, by_row)]
            arrive(piece, sems["row_all"] + d - 1)
        piece = total.at[span(mine, half)]
        send(piece, piece, sems["pair_all"], at(row, mate))
        if not last:
            halo_on(step + 1)
        arrive(total.at[span(theirs, half)], sems["pair_all"])

        squares = jnp.zeros((8, LANES), F32)
        for i in range(4 * side // LANES):
            one = total[i * LANES : (i + 1) * LANES, :]
            squares += jnp.sum((one * one).reshape(LANES // 8, 8, LANES), axis=0)
        mean = jnp.sum(squares, keepdims=True) / (4 * side * LANES)
        scale = lax.rsqrt(mean + 1e-06)
        for ch in range(2):
            for j in range(2):
                at_row = (2 * ch + j) * side
                changed = probe[at_row : at_row + side, :] + total[at_row : at_row + side, :] * scale
                if last:
                    probe_end[ch, :, j * LANES : (j + 1) * LANES] = changed
                else:
                    probe[at_row : at_row + side, :] = changed

    parting = pltpu.make_async_copy(probe_end, probe_out, out_sem.at[1])
    parting.start()
    for cond, moved in started:
        when(cond, moved.wait_send)
    leaving.wait()
    parting.wait()


def on_device(rows, cols, patterns, background, offsets, probe_wave, object_field):
    side = probe_wave.shape[-1]
    margin = side // 2
    wide = 3 * margin
    pos_rows, pos_cols = patterns.shape[0], patterns.shape[1]
    positions = pos_rows * pos_cols
    assert object_field.shape[1:] == (margin, LANES) and margin == LANES
    assert side == 2 * LANES and pos_rows * STEP == margin and pos_cols * STEP == LANES
    half, pairs, by_row, by_pair, _, _, count = plan(rows, cols, side)
    tables = dft_parts(side)
    scratch = [
        pltpu.VMEM((positions, side, side), F32),
        pltpu.VMEM((positions, 2, 3, wide + margin, LANES), F32),
        pltpu.VMEM((positions, 3, wide + margin, LANES), F32),
        pltpu.VMEM((2, side, side), F32),
        pltpu.VMEM((2 * side, side), BF16),
        pltpu.VMEM((side, 2 * side), BF16),
        pltpu.VMEM((side, 2 * side), F32),
        pltpu.VMEM((4 * side, LANES), F32),
        pltpu.VMEM(patterns.shape, F32),
        pltpu.VMEM(background.shape, F32),
        pltpu.SMEM(offsets.shape, jnp.int32),
        pltpu.VMEM(probe_wave.shape, F32),
        pltpu.VMEM(tables.shape, F32),
        pltpu.VMEM((2 * side, 2 * side), BF16),
        pltpu.VMEM((2 * side, 2 * side), BF16),
        pltpu.SemaphoreType.DMA((6,)),
        pltpu.VMEM(object_field.shape, F32),
        pltpu.VMEM(probe_wave.shape, F32),
        pltpu.SemaphoreType.DMA((2,)),
    ]
    for _ in range(ITERS):
        scratch += [
            pltpu.VMEM((2, 3, wide, LANES), F32),
            pltpu.VMEM((3, 3, wide, LANES), F32),
            pltpu.VMEM((2, 3, wide, LANES), F32),
            pltpu.VMEM((2, 3, margin, LANES), F32),
            pltpu.VMEM((4 * side, LANES), F32),
            pltpu.VMEM((half, LANES), F32),
            pltpu.VMEM((rows - 1, by_row, LANES), F32),
            pltpu.VMEM((pairs - 1, by_pair, LANES), F32),
            pltpu.VMEM((4 * side, LANES), F32),
            pltpu.SemaphoreType.DMA((count,)),
            pltpu.SemaphoreType.DMA((count,)),
        ]
    in_hbm = pl.BlockSpec(memory_space=pltpu.HBM)
    return pl.pallas_call(
        functools.partial(kernel, rows, cols, pos_rows, pos_cols, side),
        out_shape=(
            jax.ShapeDtypeStruct(object_field.shape, F32),
            jax.ShapeDtypeStruct(probe_wave.shape, F32),
        ),
        in_specs=[in_hbm] * 6,
        out_specs=(in_hbm, in_hbm),
        scratch_shapes=scratch,
        compiler_params=pltpu.CompilerParams(
            collective_id=0, has_side_effects=True, vmem_limit_bytes=60 * 1024 * 1024
        ),
    )(patterns, background, offsets, probe_wave, object_field, jnp.asarray(tables))


def solution(mesh):
    placed = (P("row", "col", None, None), P(), P("row", "col", None), P(), P(None, "row", "col"))
    return jax.shard_map(
        functools.partial(on_device, mesh.shape["row"], mesh.shape["col"]),
        mesh=mesh,
        in_specs=placed,
        out_specs=(P(None, "row", "col"), P()),
        check_vma=False,
    )
```

time: 570 us -> 96.2 us (0.17)
  waiting for transfers between devices: 270 us -> 0 us
  local copies, waits for them, and re-layouts: 151 us -> 3.44 us
  Pallas kernels: 0 us -> 91.9 us
  starting transfers between devices: 40.7 us -> 0 us
  other arithmetic: 39 us -> 0 us
  loops' own time: 29.7 us -> 0 us
  matrix products: 19.9 us -> 0 us
  between operations: 16 us -> 0.64 us
    psum x2 -> x0, waiting for transfers between devices: 242 us -> none  [on_device(): summed = lax.psum(probe_terms, ('row', 'col'))]
    pallas_call x0 -> x1, Pallas kernels: none -> 91.9 us  [on_device(): pl.pallas_call(functools.partial(kernel, rows, cols, pos_rows, pos_cols,...]
    dynamic_update_slice x8 -> x0, local copies, waits for them, and re-layouts: 90 us -> none  [add_window(): lax.dynamic_update_slice(accumulated, current + obj_term, (channel_zero,...]
    ppermute x16 -> x0, starting transfers between devices: 40.6 us -> none  [the longest x8 26.6 us: extended(): before = lax.ppermute(last, axis, up)]
    another operation x4 -> x0, loops' own time: 29.7 us -> none  [the longest x2 29.4 us: on_device(): lax.fori_loop(0, pos_count, add_window, jnp.zeros((3, widened.shape[1], w...]
    ppermute x16 -> x0, waiting for transfers between devices: 28.7 us -> none  [the longest x8 22.7 us: extended(): after = lax.ppermute(first, axis, down)]
    gather x40 -> x0, local copies, waits for them, and re-layouts: 27.8 us -> none
    dot_general x4 -> x0, matrix products: 19.9 us -> none  [transform(): jnp.einsum('pckn,cdnm->pdkm', half_way, right_table, preferred_element_ty...]
  transfers between devices with their start and end apart: 18 -> 0, of which waited for: 12 -> 0; matrix products, arithmetic and copies ran while one was open for 4% -> 0% of each run, Pallas kernels for 0% -> 0%
where the time goes in v1:
time: 96.2 us; the launch traced here: 96 us
  Pallas kernels  91.9 us (96%)
  local copies, waits for them, and re-layouts  3.44 us (4%)
    pallas_call x1, Pallas kernels, on_device(): pl.pallas_call(functools.partial(kernel, rows, cols, pos_rows, pos_cols,...  91.9 us
    unnamed x2, local copies, waits for them, and re-layouts  3.44 us

profile of v1, /device:TPU:1, one launch (start us, length us, event | category | flops | bytes accessed | tf_op | source)
XLA Modules:
  0.0 96.0 jit_solution(14502177291816367300)
XLA Ops:
  0.6 91.9 %shard_map.77 = (f32[2,128,128]{2,1,0:T(8,128)}, f32[2,256,256]{2,1,0:T(8,128)}) custom-call(f32[2,2,256,256]{3,2,1,0:T(8,128)} %refs_0_.1, f32[256,256]{1,0:T(8,128)} %refs_1_.1, s32[2,2,2]{2,1,0:T(2,128)} %refs_2_.1, f32[2,256,256]{2,1,0:T(8,128)} %refs_3_.1, f32[2,128,128]{2,1,0:T(8,128)} %refs_4_.1, f32[2,256,256]{2,1,0:T(8,128)} %constant.2.clone.refs_5_), custom_call_target="tpu_custom_call" | custom-call | tf_op jit(solution)/shard_map/pallas_call | solution.py:517
  92.5 1.6 %copy.10 = f32[2,128,128]{2,1,0:T(8,128)} copy(f32[2,128,128]{2,1,0:T(8,128)} %get-tuple-element.4) | data formatting | bytes 262144
  94.1 1.9 %copy.11 = f32[2,256,256]{2,1,0:T(8,128)} copy(f32[2,256,256]{2,1,0:T(8,128)} %get-tuple-element.5) | data formatting | bytes 1048576

commit v2 on v1

--- a/solution.py
+++ b/solution.py
@@ -203,12 +203,16 @@
             halo_out(step)
 
         if step == 0:
-            for i in (0, 1, 2, 3):
+            for i in (2, 3):
                 fetches[i].wait()
             for ch in range(2):
                 for j in range(2):
                     at_row = (2 * ch + j) * side
                     probe[at_row : at_row + side, :] = probe_in[ch, :, j * LANES : (j + 1) * LANES]
+
+            halo_on(step)
+            for i in (0, 1):
+                fetches[i].wait()
 
             @pl.loop(0, positions)
             def _(p):
@@ -222,18 +226,17 @@
 
         chunk = 32
 
-        @pl.loop(0, positions * (side // chunk))
+        @pl.loop(0, side // chunk)
         def _(i):
-            p = lax.div(i, side // chunk)
-            r = lax.rem(i, side // chunk) * chunk
-            _, c0 = starts(p)
+            r = i * chunk
             light = []
             for j in range(2):
                 pr = probe[pl.ds(pl.multiple_of(j * side + r, chunk), chunk), :]
                 pi = probe[pl.ds(pl.multiple_of((2 + j) * side + r, chunk), chunk), :]
                 light.append(pr * pr + pi * pi)
-            for j, part in enumerate(spread_lanes(light[0], light[1], c0)):
-                lpad[p, j, pl.ds(pl.multiple_of(margin + r, chunk), chunk), :] = part
+            for p in range(positions):
+                for j, part in enumerate(spread_lanes(light[0], light[1], starts(p)[1])):
+                    lpad[p, j, pl.ds(pl.multiple_of(margin + r, chunk), chunk), :] = part
 
         def gather(source, to):
             row_starts = [starts(p)[0] for p in range(positions)]
@@ -278,7 +281,6 @@
         fold_cols(2)
 
         if step == 0:
-            halo_on(step)
             fetches[5].wait()
             real, imag = tables[0].astype(BF16), tables[1].astype(BF16)
             less = (-tables[1]).astype(BF16)
@@ -295,18 +297,14 @@
         fold_rows(2)
 
         def probe_part(ch, j, r):
-            return probe[pl.ds(pl.multiple_of((2 * ch + j) * side + r, chunk), chunk), :]
-
-        @pl.loop(0, positions)
-        def _(p):
+            at_row = (2 * ch + j) * side + r
+            return probe[at_row : at_row + chunk, :]
+
+        def leave(p, q):
             r0, c0 = starts(p)
-
-            @pl.loop(0, side // chunk)
-            def _(i):
-                r = i * chunk
-                rs = pl.ds(pl.multiple_of(r, chunk), chunk)
-                inside = lane_index(chunk) < LANES - c0
-                turn = lax.rem(2 * LANES - c0, LANES)
+            inside = lane_index(chunk) < LANES - c0
+            turn = lax.rem(2 * LANES - c0, LANES)
+            for r in range(0, side, chunk):
                 parts = []
                 for ch in range(2):
                     b = [
@@ -318,52 +316,61 @@
                     wr, wi = parts[0][j], parts[1][j]
                     pr, pi = probe_part(0, j, r), probe_part(1, j, r)
                     lanes = slice(j * LANES, (j + 1) * LANES)
-                    win[0, rs, lanes] = wr
-                    win[1, rs, lanes] = wi
-                    exit_b[rs, lanes] = (pr * wr - pi * wi).astype(BF16)
-                    ri = pl.ds(pl.multiple_of(side + r, chunk), chunk)
-                    exit_b[ri, lanes] = (pr * wi + pi * wr).astype(BF16)
-
-            def transform(one, two):
-                halfway = jnp.dot(one[...], exit_b[...], preferred_element_type=F32).astype(BF16)
-                half_b[:, 0:side] = halfway[0:side]
-                half_b[:, side : 2 * side] = halfway[side : 2 * side]
-                far[...] = jnp.dot(half_b[...], two[...], preferred_element_type=F32)
-
-            transform(left, right)
-
-            @pl.loop(0, side // chunk)
-            def _(i):
-                r = i * chunk
-                rs = pl.ds(pl.multiple_of(r, chunk), chunk)
-                fr, fi = far[rs, 0:side], far[rs, side : 2 * side]
-                scale = amp[p, rs, :] * lax.rsqrt(jnp.maximum(fr * fr + fi * fi, 0.25))
-                exit_b[rs, :] = (fr * scale).astype(BF16)
-                ri = pl.ds(pl.multiple_of(side + r, chunk), chunk)
-                exit_b[ri, :] = (fi * scale).astype(BF16)
-
-            transform(right, left)
-
-            @pl.loop(0, side // chunk)
-            def _(i):
-                r = i * chunk
-                rs = pl.ds(pl.multiple_of(r, chunk), chunk)
-                terms = [[], []]
+                    win[q, 0, r : r + chunk, lanes] = wr
+                    win[q, 1, r : r + chunk, lanes] = wi
+                    exit_b[q, r : r + chunk, lanes] = (pr * wr - pi * wi).astype(BF16)
+                    exit_b[q, side + r : side + r + chunk, lanes] = (pr * wi + pi * wr).astype(BF16)
+
+        def transform(one, two, q):
+            halfway = jnp.dot(one[...], exit_b[q], preferred_element_type=F32).astype(BF16)
+            half_b[q, :, 0:side] = halfway[0:side]
+            half_b[q, :, side : 2 * side] = halfway[side : 2 * side]
+            far[q] = jnp.dot(half_b[q], two[...], preferred_element_type=F32)
+
+        def project(p, q):
+            for r in range(0, side, chunk):
+                fr, fi = far[q, r : r + chunk, 0:side], far[q, r : r + chunk, side : 2 * side]
+                scale = amp[p, r : r + chunk, :] * lax.rsqrt(jnp.maximum(fr * fr + fi * fi, 0.25))
+                exit_b[q, r : r + chunk, :] = (fr * scale).astype(BF16)
+                exit_b[q, side + r : side + r + chunk, :] = (fi * scale).astype(BF16)
+
+        def collect(places):
+            for r in range(0, side, chunk):
+                rs = slice(r, r + chunk)
+                terms = [[[], []] for _ in places]
                 for j in range(2):
                     lanes = slice(j * LANES, (j + 1) * LANES)
-                    wr, wi = win[0, rs, lanes], win[1, rs, lanes]
                     pr, pi = probe_part(0, j, r), probe_part(1, j, r)
-                    dr = far[rs, j * LANES : (j + 1) * LANES] - (pr * wr - pi * wi)
-                    di = far[rs, side + j * LANES : side + (j + 1) * LANES] - (pr * wi + pi * wr)
-                    terms[0].append(pr * dr + pi * di)
-                    terms[1].append(pr * di - pi * dr)
-                    to_r = pl.ds(pl.multiple_of(j * side + r, chunk), chunk)
-                    to_i = pl.ds(pl.multiple_of((2 + j) * side + r, chunk), chunk)
-                    grad[to_r, :] += wr * dr + wi * di
-                    grad[to_i, :] += wr * di - wi * dr
-                for ch in range(2):
-                    for j, part in enumerate(spread_lanes(terms[ch][0], terms[ch][1], c0)):
-                        pad[p, ch, j, pl.ds(pl.multiple_of(margin + r, chunk), chunk), :] = part
+                    sums = [0.0, 0.0]
+                    for p, q in places:
+                        wr, wi = win[q, 0, rs, lanes], win[q, 1, rs, lanes]
+                        dr = far[q, rs, lanes] - (pr * wr - pi * wi)
+                        di = far[q, rs, side + j * LANES : side + (j + 1) * LANES]
+                        di = di - (pr * wi + pi * wr)
+                        terms[q][0].append(pr * dr + pi * di)
+                        terms[q][1].append(pr * di - pi * dr)
+                        sums[0] += wr * dr + wi * di
+                        sums[1] += wr * di - wi * dr
+                    for ch in range(2):
+                        at_row = (2 * ch + j) * side + r
+                        grad[at_row : at_row + chunk, :] += sums[ch]
+                for p, q in places:
+                    c0 = starts(p)[1]
+                    for ch in range(2):
+                        for j, part in enumerate(spread_lanes(terms[q][ch][0], terms[q][ch][1], c0)):
+                            pad[p, ch, j, margin + r : margin + r + chunk, :] = part
+
+        @pl.loop(0, positions // 2)
+        def _(i):
+            places = [(2 * i + q, q) for q in range(2)]
+            for p, q in places:
+                leave(p, q)
+            for p, q in places:
+                transform(left, right, q)
+                project(p, q)
+            for p, q in places:
+                transform(right, left, q)
+            collect(places)
 
         def span(start, size):
             return pl.ds(pl.multiple_of(start, 8), size)
@@ -475,17 +482,17 @@
     pos_rows, pos_cols = patterns.shape[0], patterns.shape[1]
     positions = pos_rows * pos_cols
     assert object_field.shape[1:] == (margin, LANES) and margin == LANES
-    assert side == 2 * LANES and pos_rows * STEP == margin and pos_cols * STEP == LANES
+    assert positions % 2 == 0 and side == 2 * LANES and pos_rows * STEP == margin and pos_cols * STEP == LANES
     half, pairs, by_row, by_pair, _, _, count = plan(rows, cols, side)
     tables = dft_parts(side)
     scratch = [
         pltpu.VMEM((positions, side, side), F32),
         pltpu.VMEM((positions, 2, 3, wide + margin, LANES), F32),
         pltpu.VMEM((positions, 3, wide + margin, LANES), F32),
-        pltpu.VMEM((2, side, side), F32),
-        pltpu.VMEM((2 * side, side), BF16),
-        pltpu.VMEM((side, 2 * side), BF16),
-        pltpu.VMEM((side, 2 * side), F32),
+        pltpu.VMEM((2, 2, side, side), F32),
+        pltpu.VMEM((2, 2 * side, side), BF16),
+        pltpu.VMEM((2, side, 2 * side), BF16),
+        pltpu.VMEM((2, side, 2 * side), F32),
         pltpu.VMEM((4 * side, LANES), F32),
         pltpu.VMEM(patterns.shape, F32),
         pltpu.VMEM(background.shape, F32),

time: 96.2 us -> 80.1 us (0.83)
  Pallas kernels: 91.9 us -> 75.8 us
    pallas_call x1, Pallas kernels: 91.9 us -> 75.8 us  [on_device(): pl.pallas_call(functools.partial(kernel, rows, cols, pos_rows, pos_cols,...]
where the time goes in v2:
time: 80.1 us; the launch traced here: 79.9 us
  Pallas kernels  75.8 us (95%)
  local copies, waits for them, and re-layouts  3.44 us (4%)
    pallas_call x1, Pallas kernels, on_device(): pl.pallas_call(functools.partial(kernel, rows, cols, pos_rows, pos_cols,...  75.8 us
    unnamed x2, local copies, waits for them, and re-layouts  3.44 us

profile of v2, /device:TPU:1, one launch (start us, length us, event | category | flops | bytes accessed | tf_op | source)
XLA Modules:
  0.0 79.9 jit_solution(8076005443605544040)
XLA Ops:
  0.6 75.8 %shard_map.77 = (f32[2,128,128]{2,1,0:T(8,128)}, f32[2,256,256]{2,1,0:T(8,128)}) custom-call(f32[2,2,256,256]{3,2,1,0:T(8,128)} %refs_0_.1, f32[256,256]{1,0:T(8,128)} %refs_1_.1, s32[2,2,2]{2,1,0:T(2,128)} %refs_2_.1, f32[2,256,256]{2,1,0:T(8,128)} %refs_3_.1, f32[2,128,128]{2,1,0:T(8,128)} %refs_4_.1, f32[2,256,256]{2,1,0:T(8,128)} %constant.2.clone.refs_5_), custom_call_target="tpu_custom_call" | custom-call | tf_op jit(solution)/shard_map/pallas_call | solution.py:524
  76.5 1.6 %copy.10 = f32[2,128,128]{2,1,0:T(8,128)} copy(f32[2,128,128]{2,1,0:T(8,128)} %get-tuple-element.4) | data formatting | bytes 262144
  78.0 1.9 %copy.11 = f32[2,256,256]{2,1,0:T(8,128)} copy(f32[2,256,256]{2,1,0:T(8,128)} %get-tuple-element.5) | data formatting | bytes 1048576

commit v3 on v2

--- a/solution.py
+++ b/solution.py
@@ -32,13 +32,13 @@
     by_row = half // rows
     by_pair = max(8, by_row // pairs)
     owners = by_row // by_pair
-    sems = {"halo": 0, "fold_col": 8, "fold_row": 14, "pair": 20}
-    sems["row_sum"] = 21
+    sems = {"halo": 0, "fold_col": 8, "fold_row": 26, "pair": 32}
+    sems["row_sum"] = 33
     sems["col_sum"] = sems["row_sum"] + rows - 1
     sems["col_all"] = sems["col_sum"] + pairs - 1
     sems["row_all"] = sems["col_all"] + pairs - 1
     sems["pair_all"] = sems["row_all"] + rows - 1
-    count = sems["pair_all"] + 1
+    count = sems["pair_all"] + rows
     return half, pairs, by_row, by_pair, owners, sems, count
 
 
@@ -238,38 +238,43 @@
                 for j, part in enumerate(spread_lanes(light[0], light[1], starts(p)[1])):
                     lpad[p, j, pl.ds(pl.multiple_of(margin + r, chunk), chunk), :] = part
 
-        def gather(source, to):
+        def gather(source, to, s):
             row_starts = [starts(p)[0] for p in range(positions)]
 
-            @pl.loop(0, wide // 64)
+            @pl.loop(0, margin // 64)
             def _(i):
-                r = i * 64
+                r = s * margin + i * 64
                 for j in range(3):
                     parts = [source(p, j, pl.ds(margin - row_starts[p] + r, 64)) for p in range(positions)]
                     acc[to, j, pl.ds(pl.multiple_of(r, 64), 64), :] = functools.reduce(
                         lambda x, y: x + y, parts
                     )
 
-        def fold_cols(ch):
-            k = sems["fold_col"] + 2 * ch
-            send(acc.at[ch, 2], got_col.at[0, ch], k, at(row, after), has_right)
-            send(acc.at[ch, 0], got_col.at[1, ch], k + 1, at(row, before), has_left)
-
-        def fold_rows(ch):
-            k = sems["fold_col"] + 2 * ch
+            rs = pl.ds(s * margin, margin)
+            k = sems["fold_col"] + 6 * to + 2 * s
+            send(acc.at[to, 2, rs], got_col.at[0, to, rs], k, at(row, after), has_right)
+            send(acc.at[to, 0, rs], got_col.at[1, to, rs], k + 1, at(row, before), has_left)
+
+        def fold_cols(ch, s):
+            rs = slice(s * margin, (s + 1) * margin)
+            k = sems["fold_col"] + 6 * ch + 2 * s
             for side_at, cond in ((0, has_left), (1, has_right)):
-                arrive(got_col.at[side_at, ch], k + side_at, cond)
+                arrive(got_col.at[side_at, ch, rs], k + side_at, cond)
 
                 @pl.when(cond)
                 def _():
-                    acc[ch, 1] += got_col[side_at, ch]
-
+                    acc[ch, 1, rs] += got_col[side_at, ch, rs]
+
+        def fold_rows(ch):
             k = sems["fold_row"] + 2 * ch
+            fold_cols(ch, 0)
+            send(acc.at[ch, 1, 0:margin], got_row.at[1, ch], k + 1, at(up, col), has_up)
+            fold_cols(ch, 2)
             send(acc.at[ch, 1, 2 * margin : wide], got_row.at[0, ch], k, at(down, col), has_down)
-            send(acc.at[ch, 1, 0:margin], got_row.at[1, ch], k + 1, at(up, col), has_up)
 
         def fold_end(ch):
             k = sems["fold_row"] + 2 * ch
+            fold_cols(ch, 1)
             for side_at, cond in ((0, has_up), (1, has_down)):
                 arrive(got_row.at[side_at, ch], k + side_at, cond)
 
@@ -277,8 +282,8 @@
                 def _():
                     acc[ch, 1, margin : 2 * margin] += got_row[side_at, ch]
 
-        gather(lambda p, j, rs: lpad[p, j, rs, :], 2)
-        fold_cols(2)
+        for s in (0, 2, 1):
+            gather(lambda p, j, rs: lpad[p, j, rs, :], 2, s)
 
         if step == 0:
             fetches[5].wait()
@@ -292,7 +297,6 @@
                 to[0:side, side : 2 * side] = two
                 to[side : 2 * side, 0:side] = three
                 to[side : 2 * side, side : 2 * side] = four
-        grad[...] = jnp.zeros_like(grad)
         halo_end(step)
         fold_rows(2)
 
@@ -353,24 +357,22 @@
                         sums[1] += wr * di - wi * dr
                     for ch in range(2):
                         at_row = (2 * ch + j) * side + r
-                        grad[at_row : at_row + chunk, :] += sums[ch]
+                        grad[at_row : at_row + chunk, :] = sums[ch]
                 for p, q in places:
                     c0 = starts(p)[1]
                     for ch in range(2):
                         for j, part in enumerate(spread_lanes(terms[q][ch][0], terms[q][ch][1], c0)):
                             pad[p, ch, j, margin + r : margin + r + chunk, :] = part
 
-        @pl.loop(0, positions // 2)
-        def _(i):
-            places = [(2 * i + q, q) for q in range(2)]
-            for p, q in places:
-                leave(p, q)
-            for p, q in places:
-                transform(left, right, q)
-                project(p, q)
-            for p, q in places:
-                transform(right, left, q)
-            collect(places)
+        places = [(p, p) for p in range(positions)]
+        for p, q in places:
+            leave(p, q)
+        for p, q in places:
+            transform(left, right, q)
+            project(p, q)
+        for p, q in places:
+            transform(right, left, q)
+        collect(places)
 
         def span(start, size):
             return pl.ds(pl.multiple_of(start, 8), size)
@@ -381,9 +383,8 @@
         owns = None if owners == pairs else group < owners
 
         send(grad.at[span(theirs, half)], got_pair, sems["pair"], at(row, mate))
-        for ch in range(2):
-            gather(lambda p, j, rs, ch=ch: pad[p, ch, j, rs, :], ch)
-            fold_cols(ch)
+        for ch, s in ((0, 0), (0, 2), (1, 0), (1, 2), (0, 1), (1, 1)):
+            gather(lambda p, j, rs, ch=ch: pad[p, ch, j, rs, :], ch, s)
         arrive(got_pair, sems["pair"])
         grad[span(mine, half), :] += got_pair[...]
 
@@ -440,17 +441,19 @@
             cond = None if owners == pairs else origin < owners
             piece = total.at[span(base_row + lax.min(origin, owners - 1) * by_pair, by_pair)]
             arrive(piece, sems["col_all"] + d - 1, cond)
+        piece = total.at[span(base_row, by_row)]
         for d in range(1, rows):
-            piece = total.at[span(base_row, by_row)]
             send(piece, piece, sems["row_all"] + d - 1, at(row_pos(d), col))
+        send(piece, piece, sems["pair_all"], at(row, mate))
         for d in range(1, rows):
             piece = total.at[span(mine + row_pos(rows - d) * by_row, by_row)]
             arrive(piece, sems["row_all"] + d - 1)
-        piece = total.at[span(mine, half)]
-        send(piece, piece, sems["pair_all"], at(row, mate))
+            send(piece, piece, sems["pair_all"] + d, at(row, mate))
         if not last:
             halo_on(step + 1)
-        arrive(total.at[span(theirs, half)], sems["pair_all"])
+        for d in range(rows):
+            piece = total.at[span(theirs + row_pos(rows - d) * by_row, by_row)]
+            arrive(piece, sems["pair_all"] + d)
 
         squares = jnp.zeros((8, LANES), F32)
         for i in range(4 * side // LANES):
@@ -475,6 +478,17 @@
     parting.wait()
 
 
+def hand_over(tile_in, probe_in, tile_out, probe_out, sem):
+    moves = [
+        pltpu.make_async_copy(tile_in, tile_out, sem.at[0]),
+        pltpu.make_async_copy(probe_in, probe_out, sem.at[1]),
+    ]
+    for move in moves:
+        move.start()
+    for move in moves:
+        move.wait()
+
+
 def on_device(rows, cols, patterns, background, offsets, probe_wave, object_field):
     side = probe_wave.shape[-1]
     margin = side // 2
@@ -482,17 +496,17 @@
     pos_rows, pos_cols = patterns.shape[0], patterns.shape[1]
     positions = pos_rows * pos_cols
     assert object_field.shape[1:] == (margin, LANES) and margin == LANES
-    assert positions % 2 == 0 and side == 2 * LANES and pos_rows * STEP == margin and pos_cols * STEP == LANES
+    assert side == 2 * LANES and pos_rows * STEP == margin and pos_cols * STEP == LANES
     half, pairs, by_row, by_pair, _, _, count = plan(rows, cols, side)
     tables = dft_parts(side)
     scratch = [
         pltpu.VMEM((positions, side, side), F32),
         pltpu.VMEM((positions, 2, 3, wide + margin, LANES), F32),
         pltpu.VMEM((positions, 3, wide + margin, LANES), F32),
-        pltpu.VMEM((2, 2, side, side), F32),
-        pltpu.VMEM((2, 2 * side, side), BF16),
-        pltpu.VMEM((2, side, 2 * side), BF16),
-        pltpu.VMEM((2, side, 2 * side), F32),
+        pltpu.VMEM((positions, 2, side, side), F32),
+        pltpu.VMEM((positions, 2 * side, side), BF16),
+        pltpu.VMEM((positions, side, 2 * side), BF16),
+        pltpu.VMEM((positions, side, 2 * side), F32),
         pltpu.VMEM((4 * side, LANES), F32),
         pltpu.VMEM(patterns.shape, F32),
         pltpu.VMEM(background.shape, F32),
@@ -521,19 +535,29 @@
             pltpu.SemaphoreType.DMA((count,)),
         ]
     in_hbm = pl.BlockSpec(memory_space=pltpu.HBM)
-    return pl.pallas_call(
+    shapes = (
+        jax.ShapeDtypeStruct(object_field.shape, F32),
+        jax.ShapeDtypeStruct(probe_wave.shape, F32),
+    )
+    limit = 60 * 1024 * 1024
+    tile, probe = pl.pallas_call(
         functools.partial(kernel, rows, cols, pos_rows, pos_cols, side),
-        out_shape=(
-            jax.ShapeDtypeStruct(object_field.shape, F32),
-            jax.ShapeDtypeStruct(probe_wave.shape, F32),
-        ),
+        out_shape=shapes,
         in_specs=[in_hbm] * 6,
         out_specs=(in_hbm, in_hbm),
         scratch_shapes=scratch,
         compiler_params=pltpu.CompilerParams(
-            collective_id=0, has_side_effects=True, vmem_limit_bytes=60 * 1024 * 1024
+            collective_id=0, has_side_effects=True, vmem_limit_bytes=limit
         ),
     )(patterns, background, offsets, probe_wave, object_field, jnp.asarray(tables))
+    return pl.pallas_call(
+        hand_over,
+        out_shape=shapes,
+        in_specs=[in_hbm] * 2,
+        out_specs=(in_hbm, in_hbm),
+        scratch_shapes=[pltpu.SemaphoreType.DMA((2,))],
+        compiler_params=pltpu.CompilerParams(vmem_limit_bytes=limit),
+    )(tile, probe)
 
 
 def solution(mesh):

time: 80.1 us -> 95.1 us (1.19)
  Pallas kernels: 75.8 us -> 94.5 us
  local copies, waits for them, and re-layouts: 3.44 us -> 0 us
    pallas_call x0 -> x1, Pallas kernels: none -> 21 us  [on_device(): pl.pallas_call(hand_over, out_shape=shapes, in_specs=[in_hbm] * 2, out_sp...]
    unnamed x2 -> x0, local copies, waits for them, and re-layouts: 3.44 us -> none
    pallas_call x1, Pallas kernels: 75.8 us -> 73.5 us  [on_device(): pl.pallas_call(functools.partial(kernel, rows, cols, pos_rows, pos_cols,...]
where the time goes in v3:
time: 95.1 us
  Pallas kernels  94.5 us (99%)
    pallas_call x1, Pallas kernels, on_device(): pl.pallas_call(functools.partial(kernel, rows, cols, pos_rows, pos_cols,...  73.5 us
    pallas_call x1, Pallas kernels, on_device(): pl.pallas_call(hand_over, out_shape=shapes, in_specs=[in_hbm] * 2, out_sp...  21 us

profile of v3, /device:TPU:1, one launch (start us, length us, event | category | flops | bytes accessed | tf_op | source)
XLA Modules:
  0.0 95.1 jit_solution(4939732865978748898)
XLA Ops:
  0.6 73.5 %shard_map.77 = (f32[2,128,128]{2,1,0:T(8,128)}, f32[2,256,256]{2,1,0:T(8,128)}) custom-call(f32[2,2,256,256]{3,2,1,0:T(8,128)} %refs_0_.1, f32[256,256]{1,0:T(8,128)} %refs_1_.1, s32[2,2,2]{2,1,0:T(2,128)} %refs_2_.1, f32[2,256,256]{2,1,0:T(8,128)} %refs_3_.1, f32[2,128,128]{2,1,0:T(8,128)} %refs_4_.1, f32[2,256,256]{2,1,0:T(8,128)} %constant.2.clone.refs_5_), custom_call_target="tpu_custom_call" | custom-call | tf_op jit(solution)/shard_map/pallas_call | solution.py:543
  74.1 21.0 %shard_map.78 = (f32[2,128,128]{2,1,0:T(8,128)}, f32[2,256,256]{2,1,0:T(8,128)}) custom-call(f32[2,128,128]{2,1,0:T(8,128)} %get-tuple-element.4.tile_in, f32[2,256,256]{2,1,0:T(8,128)} %get-tuple-element.5.probe_in), custom_call_target="tpu_custom_call" | custom-call | tf_op jit(solution)/shard_map/pallas_call | solution.py:553

commit v4 on v3

--- a/solution.py
+++ b/solution.py
@@ -60,7 +60,7 @@
     has_left, has_right = col > 0, col < cols - 1
     up, down = lax.max(row - 1, 0), lax.min(row + 1, rows - 1)
     before, after = lax.max(col - 1, 0), lax.min(col + 1, cols - 1)
-    started = []
+    started = [[] for _ in range(ITERS)]
 
     def at(r, c):
         return {"row": r, "col": c}
@@ -151,12 +151,18 @@
         def send(src, dst, k, device, cond=None):
             moved = copy(src, dst, k, device)
             when(cond, moved.start)
-            started.append((cond, moved))
+            started[step].append((cond, moved))
 
         def arrive(dst, k, cond=None):
             when(cond, copy(dst, dst, k, at(row, mate)).wait_recv)
 
         return send, arrive
+
+    def drain(step, leave=0):
+        ready = len(started[step]) - leave
+        for cond, moved in started[step][:ready]:
+            when(cond, moved.wait_send)
+        del started[step][:ready]
 
     def thirds(step):
         return lambda j, s: per_iter[step][0].at[:, j, s * margin : (s + 1) * margin, :]
@@ -210,7 +216,6 @@
                     at_row = (2 * ch + j) * side
                     probe[at_row : at_row + side, :] = probe_in[ch, :, j * LANES : (j + 1) * LANES]
 
-            halo_on(step)
             for i in (0, 1):
                 fetches[i].wait()
 
@@ -223,6 +228,18 @@
                     lpad[p, :, lo : lo + margin, :] = edge
                     for ch in range(2):
                         pad[p, ch, :, lo : lo + margin, :] = edge
+
+            fetches[5].wait()
+            real, imag = tables[0].astype(BF16), tables[1].astype(BF16)
+            less = (-tables[1]).astype(BF16)
+            for to, (one, two, three, four) in (
+                (left, (real, less, imag, real)),
+                (right, (real, imag, less, real)),
+            ):
+                to[0:side, 0:side] = one
+                to[0:side, side : 2 * side] = two
+                to[side : 2 * side, 0:side] = three
+                to[side : 2 * side, side : 2 * side] = four
 
         chunk = 32
 
@@ -282,23 +299,14 @@
                 def _():
                     acc[ch, 1, margin : 2 * margin] += got_row[side_at, ch]
 
+        if step == 0:
+            halo_on(step)
         for s in (0, 2, 1):
             gather(lambda p, j, rs: lpad[p, j, rs, :], 2, s)
 
-        if step == 0:
-            fetches[5].wait()
-            real, imag = tables[0].astype(BF16), tables[1].astype(BF16)
-            less = (-tables[1]).astype(BF16)
-            for to, (one, two, three, four) in (
-                (left, (real, less, imag, real)),
-                (right, (real, imag, less, real)),
-            ):
-                to[0:side, 0:side] = one
-                to[0:side, side : 2 * side] = two
-                to[side : 2 * side, 0:side] = three
-                to[side : 2 * side, side : 2 * side] = four
+        if step > 0:
+            drain(step - 1)
         halo_end(step)
-        fold_rows(2)
 
         def probe_part(ch, j, r):
             at_row = (2 * ch + j) * side + r
@@ -370,6 +378,7 @@
         for p, q in places:
             transform(left, right, q)
             project(p, q)
+        fold_rows(2)
         for p, q in places:
             transform(right, left, q)
         collect(places)
@@ -451,6 +460,8 @@
             send(piece, piece, sems["pair_all"] + d, at(row, mate))
         if not last:
             halo_on(step + 1)
+        if last:
+            drain(step, rows)
         for d in range(rows):
             piece = total.at[span(theirs + row_pos(rows - d) * by_row, by_row)]
             arrive(piece, sems["pair_all"] + d)
@@ -472,20 +483,26 @@
 
     parting = pltpu.make_async_copy(probe_end, probe_out, out_sem.at[1])
     parting.start()
-    for cond, moved in started:
-        when(cond, moved.wait_send)
+    drain(ITERS - 1)
     leaving.wait()
     parting.wait()
 
 
-def hand_over(tile_in, probe_in, tile_out, probe_out, sem):
-    moves = [
-        pltpu.make_async_copy(tile_in, tile_out, sem.at[0]),
-        pltpu.make_async_copy(probe_in, probe_out, sem.at[1]),
+def hand_over(tile_in, probe_in, tile_out, probe_out, tile, probe, sem):
+    entering = [
+        pltpu.make_async_copy(probe_in, probe, sem.at[0]),
+        pltpu.make_async_copy(tile_in, tile, sem.at[1]),
     ]
-    for move in moves:
+    leaving = [
+        pltpu.make_async_copy(probe, probe_out, sem.at[2]),
+        pltpu.make_async_copy(tile, tile_out, sem.at[3]),
+    ]
+    for move in entering:
         move.start()
-    for move in moves:
+    for move, onward in zip(entering, leaving):
+        move.wait()
+        onward.start()
+    for move in leaving:
         move.wait()
 
 
@@ -555,7 +572,11 @@
         out_shape=shapes,
         in_specs=[in_hbm] * 2,
         out_specs=(in_hbm, in_hbm),
-        scratch_shapes=[pltpu.SemaphoreType.DMA((2,))],
+        scratch_shapes=[
+            pltpu.VMEM(object_field.shape, F32),
+            pltpu.VMEM(probe_wave.shape, F32),
+            pltpu.SemaphoreType.DMA((4,)),
+        ],
         compiler_params=pltpu.CompilerParams(vmem_limit_bytes=limit),
     )(tile, probe)
 

time: 95.1 us -> 74.3 us (0.78)
  Pallas kernels: 94.5 us -> 73.1 us
    pallas_call x1, Pallas kernels: 21 us -> 1.9 us  [on_device(): pl.pallas_call(hand_over, out_shape=shapes, in_specs=[in_hbm] * 2, out_sp...]
    pallas_call x1, Pallas kernels: 73.5 us -> 71.2 us  [on_device(): pl.pallas_call(functools.partial(kernel, rows, cols, pos_rows, pos_cols,...]
where the time goes in v4:
time: 74.3 us; the launch traced here: 73.7 us
  Pallas kernels  73.1 us (98%)
    pallas_call x1, Pallas kernels, on_device(): pl.pallas_call(functools.partial(kernel, rows, cols, pos_rows, pos_cols,...  71.2 us
    pallas_call x1, Pallas kernels, on_device(): pl.pallas_call(hand_over, out_shape=shapes, in_specs=[in_hbm] * 2, out_sp...  1.9 us

profile of v4, /device:TPU:1, one launch (start us, length us, event | category | flops | bytes accessed | tf_op | source)
XLA Modules:
  0.0 73.7 jit_solution(11295802767975339235)
XLA Ops:
  0.6 71.2 %shard_map.77 = (f32[2,128,128]{2,1,0:T(8,128)}, f32[2,256,256]{2,1,0:T(8,128)}) custom-call(f32[2,2,256,256]{3,2,1,0:T(8,128)} %refs_0_.1, f32[256,256]{1,0:T(8,128)} %refs_1_.1, s32[2,2,2]{2,1,0:T(2,128)} %refs_2_.1, f32[2,256,256]{2,1,0:T(8,128)} %refs_3_.1, f32[2,128,128]{2,1,0:T(8,128)} %refs_4_.1, f32[2,256,256]{2,1,0:T(8,128)} %constant.2.clone.refs_5_), custom_call_target="tpu_custom_call" | custom-call | tf_op jit(solution)/shard_map/pallas_call | solution.py:560
  71.8 1.9 %shard_map.78 = (f32[2,128,128]{2,1,0:T(8,128)}, f32[2,256,256]{2,1,0:T(8,128)}) custom-call(f32[2,128,128]{2,1,0:T(8,128)} %get-tuple-element.4.tile_in, f32[2,256,256]{2,1,0:T(8,128)} %get-tuple-element.5.probe_in), custom_call_target="tpu_custom_call" | custom-call | tf_op jit(solution)/shard_map/pallas_call | solution.py:570

commit v5 on v4

--- a/solution.py
+++ b/solution.py
@@ -392,7 +392,7 @@
         owns = None if owners == pairs else group < owners
 
         send(grad.at[span(theirs, half)], got_pair, sems["pair"], at(row, mate))
-        for ch, s in ((0, 0), (0, 2), (1, 0), (1, 2), (0, 1), (1, 1)):
+        for ch, s in ((0, 0), (0, 2), (1, 0), (1, 2)):
             gather(lambda p, j, rs, ch=ch: pad[p, ch, j, rs, :], ch, s)
         arrive(got_pair, sems["pair"])
         grad[span(mine, half), :] += got_pair[...]
@@ -400,6 +400,8 @@
         for d in range(1, rows):
             piece = grad.at[span(mine + row_pos(d) * by_row, by_row)]
             send(piece, got_rows.at[d - 1], sems["row_sum"] + d - 1, at(row_pos(d), col))
+        for ch in range(2):
+            gather(lambda p, j, rs, ch=ch: pad[p, ch, j, rs, :], ch, 1)
         fold_rows(0)
         for d in range(1, rows):
             arrive(got_rows.at[d - 1], sems["row_sum"] + d - 1)

time: 74.3 us -> 73.9 us (level)
  no operation moved by 1% of the time
where the time goes in v5:
time: 73.9 us; the launch traced here: 73.7 us
  Pallas kernels  73 us (99%)
    pallas_call x1, Pallas kernels, on_device(): pl.pallas_call(functools.partial(kernel, rows, cols, pos_rows, pos_cols,...  71.1 us
    pallas_call x1, Pallas kernels, on_device(): pl.pallas_call(hand_over, out_shape=shapes, in_specs=[in_hbm] * 2, out_sp...  1.9 us

profile of v5, /device:TPU:1, one launch (start us, length us, event | category | flops | bytes accessed | tf_op | source)
XLA Modules:
  0.0 73.7 jit_solution(5850089631356709873)
XLA Ops:
  0.6 71.1 %shard_map.77 = (f32[2,128,128]{2,1,0:T(8,128)}, f32[2,256,256]{2,1,0:T(8,128)}) custom-call(f32[2,2,256,256]{3,2,1,0:T(8,128)} %refs_0_.1, f32[256,256]{1,0:T(8,128)} %refs_1_.1, s32[2,2,2]{2,1,0:T(2,128)} %refs_2_.1, f32[2,256,256]{2,1,0:T(8,128)} %refs_3_.1, f32[2,128,128]{2,1,0:T(8,128)} %refs_4_.1, f32[2,256,256]{2,1,0:T(8,128)} %constant.2.clone.refs_5_), custom_call_target="tpu_custom_call" | custom-call | tf_op jit(solution)/shard_map/pallas_call | solution.py:562
  71.8 1.9 %shard_map.78 = (f32[2,128,128]{2,1,0:T(8,128)}, f32[2,256,256]{2,1,0:T(8,128)}) custom-call(f32[2,128,128]{2,1,0:T(8,128)} %get-tuple-element.4.tile_in, f32[2,256,256]{2,1,0:T(8,128)} %get-tuple-element.5.probe_in), custom_call_target="tpu_custom_call" | custom-call | tf_op jit(solution)/shard_map/pallas_call | solution.py:572
